TPU v7x, 32 devices: a whole 2x2x4 slice. The times are simulated.
32 devices in a mesh: gx: 8 (over y, x, core), gy: 4 (over z).
Axes of the slice: x: 2, y: 2, z: 4, core: 2. Of those that a mesh axis runs over, the one named last changes fastest.
Arguments:
- fine: bfloat16 [1024, 8, 256, 128], P(('gx', 'gy')), may hold values from -1500 to 1500
- patch_count: int32 [32], P(('gx', 'gy')), may hold values from 0 to 32, as said below
- block_place: int32 [32, 16], P(('gx', 'gy')), may hold values from 0 to 15, each once within a row
Outputs:
- factor: float32 [128, 128], replicated
- modes: bfloat16 [131072, 128], P(('gx', 'gy'))
Inputs may be any that keep to these rules, and one draw needn't show every extreme that they name: `patch_count`: devices 2k and 2k + 1 in the numbering d = (index along gx) * 4 + (index along gy) hold 32 patches together; in every draw some even device holds 32 and some odd device holds 32.
All inputs are finite; a program needn't handle non-finite values.
Results may differ from a plain program's by a relative error of at most 0.004.
The roundings to bfloat16 on the way count: a program that leaves them out, or rounds other values in their place, can miss the bound.
Values may be sent and summed in bfloat16 or wider, within the bound.
A program may use at most 64 MiB of HBM per device.

v0:
```python
import jax
import jax.numpy as jnp
from jax import lax
from jax.sharding import PartitionSpec as P


def swapped(value, axis, apart):
    mask = 2**apart
    pairs = [(source, source ^ mask) for source in range(lax.axis_size(axis))]
    return lax.ppermute(value, axis, pairs)


def restrict_block(fine_block):
    return (jnp.sum(fine_block, axis=1, dtype=jnp.float32) * 0.125).astype(jnp.bfloat16)


def pick_rows(own_rows, moved_rows, wanted, slot_total):
    from_own = jnp.take(own_rows, jnp.clip(wanted, 0, slot_total - 1), axis=0)
    from_moved = jnp.take(
        moved_rows, jnp.clip(wanted - slot_total, 0, moved_rows.shape[0] - 1), axis=0
    )
    is_own = (wanted < slot_total).reshape((-1,) + (1,) * (own_rows.ndim - 1))
    return jnp.where(is_own, from_own, from_moved)


def lower_factor(gram):
    width = gram.shape[0]
    index_col = jnp.arange(width, dtype=jnp.int32)

    def column_step(column, lower):
        partial_col = gram[:, column] - jnp.dot(
            lower, lower[column], precision=lax.Precision.HIGHEST
        )
        pivot = jnp.sqrt(partial_col[column])
        values = jnp.where(
            index_col > column, partial_col / pivot, jnp.where(index_col == column, pivot, 0.0)
        )
        marker = (index_col == column).astype(jnp.float32)
        return lower + values[:, None] * marker[None, :]

    return lax.fori_loop(0, width, column_step, jnp.zeros((width, width), jnp.float32))


def lower_inverse(lower):
    width = lower.shape[0]
    index_col = jnp.arange(width, dtype=jnp.int32)
    identity = jnp.eye(width, dtype=jnp.float32)

    def row_step(row, inverse):
        known = jnp.where(index_col < row, lower[row], 0.0)
        values = (identity[row] - jnp.dot(known, inverse, precision=lax.Precision.HIGHEST)) / lower[
            row, row
        ]
        marker = (index_col == row).astype(jnp.float32)
        return inverse + marker[:, None] * values[None, :]

    return lax.fori_loop(0, width, row_step, jnp.zeros((width, width), jnp.float32))


def upper_factor(gram):
    return lower_factor(gram).T


def shards(fine, patch_count, block_place):
    slot_total = fine.shape[0]
    blocks = slot_total // 2
    patch_cells = fine.shape[2]
    width = fine.shape[3]
    parity = lax.axis_index("gy") % 2
    held_count = patch_count[0]
    excess = jnp.where(parity == 0, held_count - blocks, blocks - held_count)
    local_ids = jnp.arange(blocks, dtype=jnp.int32)
    even_index = jnp.where(
        local_ids < blocks + excess, local_ids, slot_total + local_ids - blocks - excess
    )
    odd_index = jnp.where(local_ids < excess, slot_total + local_ids, local_ids - excess)
    chosen_index = jnp.where(parity == 0, even_index, odd_index)
    ordering = jnp.take(chosen_index, block_place[0], axis=0)
    send_first = (1 - parity) * blocks
    averaged = restrict_block(fine)
    outgoing = lax.dynamic_slice_in_dim(averaged, send_first, blocks, 0)
    incoming = swapped(outgoing, "gy", 0)
    coarse = pick_rows(averaged, incoming, ordering, slot_total)
    coarse_rows = coarse.reshape(blocks * patch_cells, width)
    row_total = coarse_rows.shape[0] * lax.axis_size("gx") * lax.axis_size("gy")
    local_gram = (
        lax.dot_general(
            coarse_rows, coarse_rows, (((0,), (0,)), ((), ())), preferred_element_type=jnp.float32
        )
        / row_total
    )
    gram = lax.psum(local_gram, ("gx", "gy"))
    factor = upper_factor(gram)
    upper_inv = lower_inverse(factor.T).T
    modes = jnp.dot(coarse_rows.astype(jnp.float32), upper_inv, precision=lax.Precision.HIGHEST)
    return (factor, modes.astype(jnp.bfloat16))


def solution(mesh):
    return jax.shard_map(
        shards,
        mesh=mesh,
        in_specs=(P(("gx", "gy"), None, None, None), P(("gx", "gy")), P(("gx", "gy"), None)),
        out_specs=(P(), P(("gx", "gy"), None)),
        check_vma=False,
    )
```

profile of v0, /device:TPU:0, one launch (start us, length us, event | category | flops | bytes accessed | tf_op | source)
XLA Modules:
  0.0 584.0 jit_solution(2623710903411148630)
XLA Ops:
  7.2 9.0 %convert_reduce_fusion = f32[32,256,128]{2,1,0:T(8,128)S(1)} fusion(bf16[32,8,256,128]{3,2,1,0:T(8,128)(2,1)} %param.7), kind=kLoop, calls=%fused_computation.31 | loop fusion | flops 15728640 | bytes 20971520 | tf_op jit(solution)/shard_map/reduce_sum | solution.py:14
  16.8 1.0 constant_dynamic-slice_fusion
  17.8 3.0 collective-permute-start
  23.3 21.0 %collective-permute-done = bf16[16,256,128]{2,1,0:T(8,128)(2,1)} collective-permute-done((bf16[16,256,128]{2,1,0:T(8,128)(2,1)}, bf16[16,256,128]{2,1,0:T(8,128)(2,1)}, u32[]{:S(2)}, u32[]{:S(2)}) %collective-permute-start) | collective-permute-done | bytes 1048608 | tf_op jit(solution)/shard_map/ppermute | solution.py:10
  44.3 2.0 gather_fusion.2
  46.3 1.5 fusion.21
  47.8 3.4 fusion.22
  51.3 115.7 %all-reduce.2.cloned.1.call-done = f32[128,128]{1,0:T(8,128)} async-done(((f32[128,128]{1,0:T(8,128)}), f32[128,128]{1,0:T(8,128)}) %all-reduce.2.cloned.1.call-update) | async-done | bytes 65552 | tf_op jit(solution)/shard_map/psum | solution.py:92
  167.0 0.9 copy.9
  167.9 212.0 %while.30 = (s32[]{:T(128)}, f32[128,128]{1,0:T(8,128)S(1)}, f32[128,128]{0,1:T(8,128)S(1)}, s32[]{:T(128)}, s32[]{:T(128)}) while((s32[]{:T(128)}, f32[128,128]{1,0:T(8,128)S(1)}, f32[128,128]{0,1:T(8,128)S(1)}, s32[]{:T(128)}, s32[]{:T(128)}) %tuple.74), condition=%wide.region_3.4_spmd.clone.clone, body=%wide.region_2.3_spmd.clone.clone.sunk | while | flops 263171 | bytes 332904 | solution.py:41
  380.7 194.5 %while.31 = (s32[]{:T(128)}, f32[128,128]{1,0:T(8,128)S(1)}, f32[128,128]{1,0:T(8,128)S(1)}, f32[128,128]{1,0:T(8,128)S(1)}, s32[]{:T(128)}, /*index=5*/s32[]{:T(128)}) while((s32[]{:T(128)}, f32[128,128]{1,0:T(8,128)S(1)}, f32[128,128]{1,0:T(8,128)S(1)}, f32[128,128]{1,0:T(8,128)S(1)}, s32[]{:T(128)}, ...), condition=%wide.region_5.6_spmd.clone.clone, body=%wide.region_4.5_spmd.clone.clone.sunk | while | flops 262915 | bytes 201824 | solution.py:57
  381.2 0.8 fusion.49
  382.8 0.8 fusion.49
  384.3 0.8 fusion.49
  385.8 0.8 fusion.49
  387.3 0.8 fusion.49
  388.8 0.8 fusion.49
  390.4 0.8 fusion.49
  391.9 0.8 fusion.49
  393.4 0.8 fusion.49
  394.9 0.8 fusion.49
  396.4 0.8 fusion.49
  398.0 0.8 fusion.49
  399.5 0.8 fusion.49
  401.0 0.8 fusion.49
  402.5 0.8 fusion.49
  404.0 0.8 fusion.49
  405.6 0.8 fusion.49
  407.1 0.8 fusion.49
  408.6 0.8 fusion.49
  410.1 0.8 fusion.49
  411.6 0.8 fusion.49
  413.2 0.8 fusion.49
  414.7 0.8 fusion.49
  416.2 0.8 fusion.49
  417.7 0.8 fusion.49
  419.2 0.8 fusion.49
  420.8 0.8 fusion.49
  422.3 0.8 fusion.49
  423.8 0.8 fusion.49
  425.3 0.8 fusion.49
  426.8 0.8 fusion.49
  428.4 0.8 fusion.49
  429.9 0.8 fusion.49
  431.4 0.8 fusion.49
  432.9 0.8 fusion.49
  434.4 0.8 fusion.49
  436.0 0.8 fusion.49
  437.5 0.8 fusion.49
  439.0 0.8 fusion.49
  440.5 0.8 fusion.49
  442.0 0.8 fusion.49
  443.6 0.8 fusion.49
  445.1 0.8 fusion.49
  446.6 0.8 fusion.49
  448.1 0.8 fusion.49
  449.6 0.8 fusion.49
  451.2 0.8 fusion.49
  452.7 0.8 fusion.49
  454.2 0.8 fusion.49
  455.7 0.8 fusion.49
  457.2 0.8 fusion.49
  458.8 0.8 fusion.49
  575.2 2.0 convolution_convert_fusion
  (1254 shorter events, 269.4 us)
Async XLA Ops:
  7.2 159.8 %all-reduce.2.cloned.1.call-start = ((), (), s32[]{:S(2)}) async-start(), calls=%async_computation | async-start | bytes 131072 | tf_op jit(solution)/shard_map/psum | solution.py:92
  16.2 5.3 copy-start
  17.8 26.5 %collective-permute-start = (bf16[16,256,128]{2,1,0:T(8,128)(2,1)}, bf16[16,256,128]{2,1,0:T(8,128)(2,1)}, u32[]{:S(2)}, u32[]{:S(2)}) collective-permute-start(bf16[16,256,128]{2,1,0:T(8,128)(2,1)} %constant_dynamic-slice_fusion), channel_id=1, source_target_pairs={{0,1},{1,0},{2,3},{3,2},{4,5},{5,4},{6,7},{7,6},{8,9},{9,8},{10,11... | collective-permute-start | bytes 3145736 | tf_op jit(solution)/shard_map/ppermute | solution.py:10
Sparse Core Ops, SparseCore 0:
  47.9 118.9 all-reduce.1
where the time goes:
time: 592 us; the launch traced here: 584 us
  local copies, waits for them, and re-layouts  163 us (28%)
  waiting for transfers between devices  137 us (23%)
  matrix products  128 us (22%)
  loops' own time  98.6 us (17%)
  other arithmetic  39.6 us (7%)
  between operations  14.9 us (3%)
    psum x1, waiting for transfers between devices, shards(): gram = lax.psum(local_gram, ('gx', 'gy'))  116 us
    dot_general x128, matrix products, row_step(): jnp.dot(known, inverse, precision=lax.Precision.HIGHEST)  102 us
    another operation x1, loops' own time, lower_factor(): lax.fori_loop(0, width, column_step, jnp.zeros((width, width), jnp.float32))  94.9 us
    dynamic_slice x128, local copies, waits for them, and re-layouts, column_step(): pivot = jnp.sqrt(partial_col[column])  81.4 us
    dynamic_slice x128, local copies, waits for them, and re-layouts, row_step(): lower[row, row]  75.2 us
    dot_general x128, matrix products, column_step(): jnp.dot(lower, lower[column], precision=lax.Precision.HIGHEST)  22.4 us
    ppermute x1, waiting for transfers between devices, swapped(): return lax.ppermute(value, axis, pairs)  21 us
    add x128, other arithmetic, row_step(): return inverse + marker[:, None] * values[None, :]  12.9 us
  transfers between devices with their start and end apart: 2, of which 2 were waited for; matrix products, arithmetic and copies ran while one was open for 1% of the time, Pallas kernels for 0%

commit v1 on v0

v1 whole, which is shorter than its diff:
```python
import functools

import jax
import jax.numpy as jnp
from jax import lax
from jax.experimental import pallas as pl
from jax.experimental.pallas import tpu as pltpu
from jax.sharding import PartitionSpec as P

MESH = pl.DeviceIdType.MESH


def average_kernel(meta_ref, fine_ref, avg_ref, gram_ref):
    step = pl.program_id(0)
    slots, children, cells, width = fine_ref.shape

    @pl.when(step == 0)
    def _():
        gram_ref[...] = jnp.zeros_like(gram_ref)

    piece = 32
    for slot in range(slots):
        valid = meta_ref[0] * meta_ref[2] + step * slots + slot < meta_ref[1]
        for row in range(0, cells, piece):
            rows = pl.ds(row, piece)
            total = fine_ref[slot, 0, rows, :].astype(jnp.float32)
            for child in range(1, children):
                total += fine_ref[slot, child, rows, :].astype(jnp.float32)
            avg_ref[slot, rows, :] = (total * (1.0 / children)).astype(jnp.bfloat16)
        weight = jnp.where(valid, 1.0, 0.0).astype(jnp.float32)
        part = avg_ref[slot]
        gram_ref[...] += weight * lax.dot_general(
            part, part, (((0,), (0,)), ((), ())), preferred_element_type=jnp.float32
        )


def average_half(fine, half, count):
    slot_total, children, cells, width = fine.shape
    blocks = slot_total // 2
    slots = 2 if blocks % 2 == 0 else 1
    steps = blocks // slots
    meta = jnp.stack([half, count, jnp.int32(blocks)])
    return pl.pallas_call(
        average_kernel,
        grid_spec=pltpu.PrefetchScalarGridSpec(
            num_scalar_prefetch=1,
            grid=(steps,),
            in_specs=[
                pl.BlockSpec(
                    (slots, children, cells, width),
                    lambda i, meta: (meta[0] * steps + i, 0, 0, 0),
                )
            ],
            out_specs=[
                pl.BlockSpec((slots, cells, width), lambda i, meta: (i, 0, 0)),
                pl.BlockSpec((width, width), lambda i, meta: (0, 0)),
            ],
        ),
        out_shape=[
            jax.ShapeDtypeStruct((blocks, cells, width), jnp.bfloat16),
            jax.ShapeDtypeStruct((width, width), jnp.float32),
        ],
        compiler_params=pltpu.CompilerParams(vmem_limit_bytes=56 * 2**20),
        cost_estimate=pl.CostEstimate(
            flops=2 * blocks * cells * width * width,
            bytes_accessed=fine.size + fine.size // children,
            transcendentals=0,
        ),
    )(meta, fine)


def sum_kernel(n_gx, n_gy, row_total, first_ref, second_ref, out_ref, local, parts, planes, send, recv):
    gx, gy = lax.axis_index("gx"), lax.axis_index("gy")
    width = out_ref.shape[0]
    rows = width // n_gx
    barrier = pltpu.get_barrier_semaphore()
    for apart in range(1, n_gx):
        pl.semaphore_signal(
            barrier, inc=1, device_id=(lax.rem(gx + apart, n_gx), gy), device_id_type=MESH
        )
    for apart in range(1, n_gy):
        pl.semaphore_signal(
            barrier, inc=1, device_id=(gx, lax.rem(gy + apart, n_gy)), device_id_type=MESH
        )
    local[...] = first_ref[...] + second_ref[...]
    pl.semaphore_wait(barrier, n_gx + n_gy - 2)

    copies = []
    for apart in range(1, n_gx):
        there = lax.rem(gx + apart, n_gx)
        copy = pltpu.make_async_remote_copy(
            src_ref=local.at[pl.ds(pl.multiple_of(there * rows, rows), rows)],
            dst_ref=parts.at[apart],
            send_sem=send.at[0, apart],
            recv_sem=recv.at[0, apart],
            device_id=(there, gy),
            device_id_type=MESH,
        )
        copy.start()
        copies.append(copy)
    total = local[pl.ds(pl.multiple_of(gx * rows, rows), rows), :]
    for apart in range(1, n_gx):
        copies[apart - 1].wait_recv()
        total += parts[apart]
    planes[gy] = total

    for apart in range(1, n_gy):
        copy = pltpu.make_async_remote_copy(
            src_ref=planes.at[gy],
            dst_ref=planes.at[gy],
            send_sem=send.at[1, apart],
            recv_sem=recv.at[1, apart],
            device_id=(gx, lax.rem(gy + apart, n_gy)),
            device_id_type=MESH,
        )
        copy.start()
        copies.append(copy)
    for apart in range(1, n_gy):
        copies[n_gx - 2 + apart].wait_recv()
    total = planes[0]
    for plane in range(1, n_gy):
        total += planes[plane]
    mine = pl.ds(pl.multiple_of(gx * rows, rows), rows)
    out_ref[mine, :] = total / row_total

    last = []
    for apart in range(1, n_gx):
        copy = pltpu.make_async_remote_copy(
            src_ref=out_ref.at[mine],
            dst_ref=out_ref.at[mine],
            send_sem=send.at[2, apart],
            recv_sem=recv.at[2, apart],
            device_id=(lax.rem(gx + apart, n_gx), gy),
            device_id_type=MESH,
        )
        copy.start()
        last.append(copy)
    for copy in copies:
        copy.wait_send()
    for copy in last:
        copy.wait()


def sum_everywhere(first, second, row_total):
    n_gx, n_gy = lax.axis_size("gx"), lax.axis_size("gy")
    width = first.shape[0]
    rows = width // n_gx
    most = max(n_gx, n_gy)
    return pl.pallas_call(
        functools.partial(sum_kernel, n_gx, n_gy, row_total),
        out_shape=jax.ShapeDtypeStruct((width, width), jnp.float32),
        in_specs=[pl.BlockSpec(memory_space=pltpu.VMEM)] * 2,
        out_specs=pl.BlockSpec(memory_space=pltpu.VMEM),
        scratch_shapes=[
            pltpu.VMEM((width, width), jnp.float32),
            pltpu.VMEM((n_gx, rows, width), jnp.float32),
            pltpu.VMEM((n_gy, rows, width), jnp.float32),
            pltpu.SemaphoreType.DMA((3, most)),
            pltpu.SemaphoreType.DMA((3, most)),
        ],
        compiler_params=pltpu.CompilerParams(collective_id=0, has_side_effects=True),
        cost_estimate=pl.CostEstimate(flops=0, bytes_accessed=32 * 2**20, transcendentals=0),
    )(first, second)


def factor_kernel(gram_ref, factor_ref, split_ref):
    width = gram_ref.shape[0]
    step = 8
    groups = width // step
    lane = lax.broadcasted_iota(jnp.int32, (step, width), 1)
    sub = lax.broadcasted_iota(jnp.int32, (step, width), 0)
    gram = [gram_ref[g * step : (g + 1) * step, :] for g in range(groups)]
    inv = [(lane == sub + g * step).astype(jnp.float32) for g in range(groups)]
    done = []
    for g in range(groups):
        base = g * step
        cols = [
            [jnp.broadcast_to(gram[h][:, base + j : base + j + 1], (step, width)) for h in range(g, groups)]
            for j in range(step)
        ]
        rows = [jnp.broadcast_to(gram[g][j : j + 1, :], (step, width)) for j in range(step)]
        irows = [jnp.broadcast_to(inv[g][j : j + 1, :], (step, width)) for j in range(step)]
        scaled = []
        upper = jnp.zeros((step, width), jnp.float32)
        lower = jnp.zeros((step, width), jnp.float32)
        for j in range(step):
            splat = [jnp.broadcast_to(cols[j][0][i : i + 1, :], (step, width)) for i in range(j, step)]
            pivot = splat[0]
            over = 1.0 / pivot
            srow, sirow = rows[j] * over, irows[j] * over
            scaled.append((srow, sirow))
            for i in range(j + 1, step):
                ratio = splat[i - j] * over
                rows[i] = rows[i] - splat[i - j] * srow
                irows[i] = irows[i] - splat[i - j] * sirow
                cols[i] = [cols[i][h] - ratio * cols[j][h] for h in range(groups - g)]
            root = lax.rsqrt(pivot)
            upper = jnp.where(sub == j, rows[j] * root, upper)
            lower = jnp.where(sub == j, irows[j] * root, lower)
        factor_ref[base : base + step, :] = jnp.where(lane >= sub + base, upper, 0.0)
        done.append(lower)
        for h in range(g + 1, groups):
            for j in range(step):
                gram[h] = gram[h] - cols[j][h - g] * scaled[j][0]
                inv[h] = inv[h] - cols[j][h - g] * scaled[j][1]
    whole = jnp.concatenate(done, axis=0).T
    high = whole.astype(jnp.bfloat16)
    split_ref[:, :width] = high
    split_ref[:, width:] = (whole - high.astype(jnp.float32)).astype(jnp.bfloat16)


def factor_and_inverse(gram):
    width = gram.shape[0]
    return pl.pallas_call(
        factor_kernel,
        out_shape=[
            jax.ShapeDtypeStruct((width, width), jnp.float32),
            jax.ShapeDtypeStruct((width, 2 * width), jnp.bfloat16),
        ],
        in_specs=[pl.BlockSpec(memory_space=pltpu.VMEM)],
        out_specs=[pl.BlockSpec(memory_space=pltpu.VMEM)] * 2,
        compiler_params=pltpu.CompilerParams(vmem_limit_bytes=32 * 2**20),
        cost_estimate=pl.CostEstimate(flops=0, bytes_accessed=32 * 2**20, transcendentals=0),
    )(gram)


def modes_kernel(which_ref, place_ref, split_ref, kept_ref, sent_ref, moved_ref, out_ref, rows, result, in_sem, out_sem):
    blocks, cells, width = rows.shape
    sources = (kept_ref, sent_ref, moved_ref)
    for block in range(blocks):
        for index, source in enumerate(sources):

            @pl.when(which_ref[block] == index)
            def _():
                pltpu.make_async_copy(
                    source.at[place_ref[block]], rows.at[block], in_sem.at[block]
                ).start()

    split = split_ref[...]
    copies = []
    for block in range(blocks):
        pltpu.make_async_copy(kept_ref.at[0], rows.at[block], in_sem.at[block]).wait()
        both = jnp.dot(rows[block], split, preferred_element_type=jnp.float32)
        result[block] = (both[:, :width] + both[:, width:]).astype(jnp.bfloat16)
        copy = pltpu.make_async_copy(
            result.at[block], out_ref.at[pl.ds(block * cells, cells)], out_sem.at[block]
        )
        copy.start()
        copies.append(copy)
    for copy in copies:
        copy.wait()


def make_modes(which, place, split, kept, sent, moved):
    blocks, cells, width = kept.shape
    any_spec = pl.BlockSpec(memory_space=pl.ANY)
    smem = pl.BlockSpec(memory_space=pltpu.SMEM)
    return pl.pallas_call(
        modes_kernel,
        out_shape=jax.ShapeDtypeStruct((blocks * cells, width), jnp.bfloat16),
        in_specs=[smem, smem, pl.BlockSpec(memory_space=pltpu.VMEM), any_spec, any_spec, any_spec],
        out_specs=any_spec,
        scratch_shapes=[
            pltpu.VMEM((blocks, cells, width), jnp.bfloat16),
            pltpu.VMEM((blocks, cells, width), jnp.bfloat16),
            pltpu.SemaphoreType.DMA((blocks,)),
            pltpu.SemaphoreType.DMA((blocks,)),
        ],
        compiler_params=pltpu.CompilerParams(vmem_limit_bytes=32 * 2**20),
        cost_estimate=pl.CostEstimate(
            flops=4 * blocks * cells * width * width,
            bytes_accessed=4 * blocks * cells * width,
            transcendentals=0,
        ),
    )(which, place, split, kept, sent, moved)


def shards(fine, patch_count, block_place):
    slot_total = fine.shape[0]
    blocks = slot_total // 2
    patch_cells = fine.shape[2]
    parity = lax.axis_index("gy") % 2
    held_count = patch_count[0]
    send_half = 1 - parity
    sent, sent_gram = average_half(fine, send_half, held_count)
    pairs = [(source, source ^ 1) for source in range(lax.axis_size("gy"))]
    moved = lax.ppermute(sent, "gy", pairs)
    kept, kept_gram = average_half(fine, parity, held_count)
    row_total = blocks * patch_cells * lax.axis_size("gx") * lax.axis_size("gy")
    gram = sum_everywhere(sent_gram, kept_gram, row_total)
    factor, split = factor_and_inverse(gram)

    excess = jnp.where(parity == 0, held_count - blocks, blocks - held_count)
    wanted = block_place[0]
    is_moved = jnp.where(parity == 0, wanted >= blocks + excess, wanted < excess)
    own = jnp.where(parity == 0, wanted, wanted - excess)
    is_sent = own // blocks == send_half
    which = jnp.where(is_moved, 2, jnp.where(is_sent, 1, 0)).astype(jnp.int32)
    moved_place = jnp.where(parity == 0, wanted - blocks - excess, wanted)
    place = jnp.where(is_moved, moved_place, own % blocks)
    place = jnp.clip(place, 0, blocks - 1).astype(jnp.int32)
    modes = make_modes(which, place, split, kept, sent, moved)
    return (factor, modes)


def solution(mesh):
    return jax.shard_map(
        shards,
        mesh=mesh,
        in_specs=(P(("gx", "gy"), None, None, None), P(("gx", "gy")), P(("gx", "gy"), None)),
        out_specs=(P(), P(("gx", "gy"), None)),
        check_vma=False,
    )
```

time: 592 us -> 58.4 us (0.10); the launches traced: 584 us -> 57.8 us
  local copies, waits for them, and re-layouts: 163 us -> 2.06 us
  waiting for transfers between devices: 137 us -> 0.01 us
  matrix products: 128 us -> 0 us
  loops' own time: 98.6 us -> 0 us
  Pallas kernels: 0 us -> 50.1 us
  other arithmetic: 39.6 us -> 1.32 us
  between operations: 14.9 us -> 1.33 us
    dynamic_slice x257 -> x0, local copies, waits for them, and re-layouts: 158 us -> none  [the longest x128 81.4 us: column_step(): pivot = jnp.sqrt(partial_col[column])]
    dot_general x258 -> x0, matrix products: 128 us -> none  [the longest x128 102 us: row_step(): jnp.dot(known, inverse, precision=lax.Precision.HIGHEST)]
    psum x1 -> x0, waiting for transfers between devices: 116 us -> none  [shards(): gram = lax.psum(local_gram, ('gx', 'gy'))]
    another operation x2 -> x0, loops' own time: 98.6 us -> none  [the longest x1 94.9 us: lower_factor(): lax.fori_loop(0, width, column_step, jnp.zeros((width, width), jnp.float32))]
    pallas_call x0 -> x5, Pallas kernels: none -> 50.1 us  [the longest x1 21.9 us: sum_everywhere(): pl.pallas_call(functools.partial(sum_kernel, n_gx, n_gy, row_total), out_...]
    add x256 -> x0, other arithmetic: 23.8 us -> none  [the longest x128 12.9 us: row_step(): return inverse + marker[:, None] * values[None, :]]
    ppermute x1, waiting for transfers between devices: 21 us -> 0.01 us  [shards(): moved = lax.ppermute(sent, 'gy', pairs)]
    reduce_sum x1 -> x0, other arithmetic: 9.01 us -> none  [restrict_block(): jnp.sum(fine_block, axis=1, dtype=jnp.float32) * 0.125]
  transfers between devices with their start and end apart: 2 -> 1, of which waited for: 2 -> 0; matrix products, arithmetic and copies ran while one was open for 1% -> 1% of each run, Pallas kernels for 0% -> 61%
where the time goes in v1:
time: 58.4 us; the launch traced here: 57.8 us
  Pallas kernels  50.1 us (86%)
  starting transfers between devices  3.02 us (5%)
  local copies, waits for them, and re-layouts  2.06 us (4%)
  between operations  1.33 us (2%)
  other arithmetic  1.32 us (2%)
    pallas_call x1, Pallas kernels, sum_everywhere(): pl.pallas_call(functools.partial(sum_kernel, n_gx, n_gy, row_total), out_...  21.9 us
    pallas_call x2, Pallas kernels, average_half(): pl.pallas_call(average_kernel, grid_spec=pltpu.PrefetchScalarGridSpec(num...  17.1 us
    pallas_call x1, Pallas kernels, make_modes(): pl.pallas_call(modes_kernel, out_shape=jax.ShapeDtypeStruct((blocks * cel...  6.42 us
    pallas_call x1, Pallas kernels, factor_and_inverse(): pl.pallas_call(factor_kernel, out_shape=[jax.ShapeDtypeStruct((width, wid...  4.63 us
    ppermute x1, starting transfers between devices, shards(): moved = lax.ppermute(sent, 'gy', pairs)  3.02 us
    unnamed x8, local copies, waits for them, and re-layouts  2.06 us
    another operation x2, other arithmetic, average_half(): meta = jnp.stack([half, count, jnp.int32(blocks)])  1.3 us
  transfers between devices with their start and end apart: 1, of which 0 were waited for; matrix products, arithmetic and copies ran while one was open for 1% of the time, Pallas kernels for 61%

profile of v1, /device:TPU:0, one launch (start us, length us, event | category | flops | bytes accessed | tf_op | source)
XLA Modules:
  0.0 57.8 jit_solution(6314032568611129867)
XLA Ops:
  1.3 0.6 %pad_add_fusion.1.meta_ref = s32[3]{0:T(128)} fusion(s32[1]{0:T(128)} %constant.48.clone.1, s32[1]{0:T(128)} %bitcast, s32[1]{0:T(128)S(6)} %copy.5), kind=kLoop, calls=%fused_computation.10 | loop fusion | flops 6 | bytes 24 | tf_op jit(solution)/shard_map/stack | solution.py:42
  1.9 0.0 copy-start.3
  1.9 8.6 %shard_map.50 = (bf16[16,256,128]{2,1,0:T(8,128)(2,1)}, f32[128,128]{1,0:T(8,128)}) custom-call(s32[3]{0:T(128)} %pad_add_fusion.1.meta_ref, bf16[32,8,256,128]{3,2,1,0:T(8,128)(2,1)} %fine_ref.3), custom_call_target="tpu_custom_call" | custom-call | flops 134217728 | bytes 9437184 | tf_op jit(solution)/shard_map/pallas_call | solution.py:43
  10.5 0.0 copy-start
  10.5 3.0 %collective-permute-start = (bf16[16,256,128]{2,1,0:T(8,128)(2,1)}, bf16[16,256,128]{2,1,0:T(8,128)(2,1)S(1)}, u32[]{:S(2)}, u32[]{:S(2)}) collective-permute-start(bf16[16,256,128]{2,1,0:T(8,128)(2,1)} %get-tuple-element.13.sent_ref), channel_id=1, source_target_pairs={{0,1},{1,0},{2,3},{3,2},{4,5},{5,4},{6,7},{7,6},{8,9},{9,8},{10,11... | collective-permute-start | bytes 3145736 | tf_op jit(solution)/shard_map/ppermute | solution.py:287
  13.6 0.7 %pad_add_fusion.meta_ref = s32[3]{0:T(128)} fusion(s32[1]{0:T(128)} %constant.48.clone.1, s32[1]{0:T(128)} %bitcast.1, s32[1]{0:T(128)S(6)} %copy.5), kind=kLoop, calls=%fused_computation.9 | loop fusion | flops 6 | bytes 24 | tf_op jit(solution)/shard_map/stack | solution.py:42
  14.2 8.5 %shard_map.51 = (bf16[16,256,128]{2,1,0:T(8,128)(2,1)}, f32[128,128]{1,0:T(8,128)}) custom-call(s32[3]{0:T(128)} %pad_add_fusion.meta_ref, bf16[32,8,256,128]{3,2,1,0:T(8,128)(2,1)} %fine_ref.3), custom_call_target="tpu_custom_call" | custom-call | flops 134217728 | bytes 9437184 | tf_op jit(solution)/shard_map/pallas_call | solution.py:43
  22.7 21.9 %shard_map.52.gram_ref = f32[128,128]{1,0:T(8,128)} custom-call(f32[128,128]{1,0:T(8,128)} %get-tuple-element.8.first_ref, f32[128,128]{1,0:T(8,128)} %get-tuple-element.9.second_ref), custom_call_target="tpu_custom_call" | custom-call | bytes 33554432 | tf_op jit(solution)/shard_map/pallas_call | solution.py:149
  44.6 0.0 copy-start.2
  44.6 0.8 %copy-done.2 = f32[128,128]{1,0:T(8,128)S(1)} copy-done((f32[128,128]{1,0:T(8,128)S(1)}, f32[128,128]{1,0:T(8,128)}, u32[]{:S(2)}) %copy-start.2) | copy-done | bytes 65560
  45.5 4.6 %shard_map.53 = (f32[128,128]{1,0:T(8,128)}, bf16[128,256]{1,0:T(8,128)(2,1)S(1)}) custom-call(f32[128,128]{1,0:T(8,128)S(1)} %copy-done.2), custom_call_target="tpu_custom_call" | custom-call | bytes 33554432 | tf_op jit(solution)/shard_map/pallas_call | solution.py:214
  50.1 0.0 copy-done.3
  50.1 0.0 collective-permute-done.moved_ref
  50.1 0.0 copy-done
  50.1 0.0 copy-start.1
  50.1 1.2 %copy-done.1 = bf16[16,256,128]{2,1,0:T(8,128)(2,1)S(1)} copy-done((bf16[16,256,128]{2,1,0:T(8,128)(2,1)S(1)}, bf16[16,256,128]{2,1,0:T(8,128)(2,1)}, u32[]{:S(2)}) %copy-start.1) | copy-done | bytes 1048600
  51.4 6.4 %shard_map.54 = bf16[4096,128]{1,0:T(8,128)(2,1)} custom-call(s32[16]{0:T(128)S(1)} %get-tuple-element.15.which_ref, s32[16]{0:T(128)S(1)} %get-tuple-element.14.place_ref, bf16[128,256]{1,0:T(8,128)(2,1)S(1)} %get-tuple-element.11.split_ref, bf16[16,256,128]{2,1,0:T(8,128)(2,1)S(1)} %copy-done.1, bf16[16,256,128]{2,1,0:T(8,128)(2,1)S(1)} %copy-done, ...), custom_call_target="tpu_custom_call" | custom-call | flops 268435456 | bytes 2097152 | tf_op jit(solution)/shard_map/pallas_call | solution.py:258
  (1 shorter events, 0.0 us)
Async XLA Ops:
  1.9 48.2 %copy-start.3 = (s32[1,16]{1,0:T(1,128)S(1)}, s32[1,16]{1,0:T(1,128)}, u32[]{:S(2)}) copy-start(s32[1,16]{1,0:T(1,128)} %param.5) | copy-start | bytes 196
  10.5 39.6 %copy-start = (bf16[16,256,128]{2,1,0:T(8,128)(2,1)S(1)}, bf16[16,256,128]{2,1,0:T(8,128)(2,1)}, u32[]{:S(2)}) copy-start(bf16[16,256,128]{2,1,0:T(8,128)(2,1)} %get-tuple-element.13.sent_ref) | copy-start | bytes 3145732
  10.5 39.6 %collective-permute-start = (bf16[16,256,128]{2,1,0:T(8,128)(2,1)}, bf16[16,256,128]{2,1,0:T(8,128)(2,1)S(1)}, u32[]{:S(2)}, u32[]{:S(2)}) collective-permute-start(bf16[16,256,128]{2,1,0:T(8,128)(2,1)} %get-tuple-element.13.sent_ref), channel_id=1, source_target_pairs={{0,1},{1,0},{2,3},{3,2},{4,5},{5,4},{6,7},{7,6},{8,9},{9,8},{10,11... | collective-permute-start | bytes 3145736 | tf_op jit(solution)/shard_map/ppermute | solution.py:287
  44.6 0.8 %copy-start.2 = (f32[128,128]{1,0:T(8,128)S(1)}, f32[128,128]{1,0:T(8,128)}, u32[]{:S(2)}) copy-start(f32[128,128]{1,0:T(8,128)} %shard_map.52.gram_ref) | copy-start | bytes 196612
  50.1 1.2 %copy-start.1 = (bf16[16,256,128]{2,1,0:T(8,128)(2,1)S(1)}, bf16[16,256,128]{2,1,0:T(8,128)(2,1)}, u32[]{:S(2)}) copy-start(bf16[16,256,128]{2,1,0:T(8,128)(2,1)} %get-tuple-element.12.kept_ref) | copy-start | bytes 3145732

commit v2 on v1

--- a/solution.py
+++ b/solution.py
@@ -10,60 +10,79 @@
 MESH = pl.DeviceIdType.MESH
 
 
-def average_kernel(meta_ref, fine_ref, avg_ref, gram_ref):
+def average_kernel(lens, meta_ref, fine_ref, *refs):
     step = pl.program_id(0)
     slots, children, cells, width = fine_ref.shape
+    outs, gram_ref, masked = refs[: len(lens)], refs[-2], refs[-1]
 
     @pl.when(step == 0)
     def _():
         gram_ref[...] = jnp.zeros_like(gram_ref)
 
-    piece = 32
-    for slot in range(slots):
-        valid = meta_ref[0] * meta_ref[2] + step * slots + slot < meta_ref[1]
-        for row in range(0, cells, piece):
-            rows = pl.ds(row, piece)
-            total = fine_ref[slot, 0, rows, :].astype(jnp.float32)
-            for child in range(1, children):
-                total += fine_ref[slot, child, rows, :].astype(jnp.float32)
-            avg_ref[slot, rows, :] = (total * (1.0 / children)).astype(jnp.bfloat16)
-        weight = jnp.where(valid, 1.0, 0.0).astype(jnp.float32)
-        part = avg_ref[slot]
-        gram_ref[...] += weight * lax.dot_general(
-            part, part, (((0,), (0,)), ((), ())), preferred_element_type=jnp.float32
-        )
-
-
-def average_half(fine, half, count):
+    def work(avg_ref):
+        piece = 32
+        acc = None
+        for slot in range(slots):
+            number = lax.rem(meta_ref[0] + step * slots + slot, meta_ref[2])
+            weight = jnp.where(number < meta_ref[1], 1.0, 0.0).astype(jnp.float32)
+            for row in range(0, cells, piece):
+                rows = pl.ds(row, piece)
+                total = fine_ref[slot, 0, rows, :].astype(jnp.float32)
+                for child in range(1, children):
+                    total += fine_ref[slot, child, rows, :].astype(jnp.float32)
+                mean = total * (1.0 / children)
+                avg_ref[slot, rows, :] = mean.astype(jnp.bfloat16)
+                masked[slot, rows, :] = (mean * weight).astype(jnp.bfloat16)
+            part = masked[slot]
+            term = lax.dot_general(
+                part, part, (((0,), (0,)), ((), ())), preferred_element_type=jnp.float32
+            )
+            acc = term if acc is None else acc + term
+        gram_ref[...] += acc
+
+    start = 0
+    for length, out in zip(lens, outs):
+        if len(lens) == 1:
+            work(out)
+        else:
+            pl.when((step >= start) & (step < start + length))(functools.partial(work, out))
+        start += length
+
+
+def average_range(fine, first, count, lens):
     slot_total, children, cells, width = fine.shape
-    blocks = slot_total // 2
-    slots = 2 if blocks % 2 == 0 else 1
-    steps = blocks // slots
-    meta = jnp.stack([half, count, jnp.int32(blocks)])
+    slots = slot_total // 8
+    total = sum(lens)
+    steps = [length // slots for length in lens]
+    starts = [sum(steps[:k]) for k in range(len(steps))]
+    meta = jnp.stack([first, count, jnp.int32(slot_total)])
+
+    def out_spec(start, length):
+        return pl.BlockSpec(
+            (slots, cells, width), lambda i, meta: (jnp.clip(i - start, 0, length - 1), 0, 0)
+        )
+
     return pl.pallas_call(
-        average_kernel,
+        functools.partial(average_kernel, steps),
         grid_spec=pltpu.PrefetchScalarGridSpec(
             num_scalar_prefetch=1,
-            grid=(steps,),
+            grid=(sum(steps),),
             in_specs=[
                 pl.BlockSpec(
                     (slots, children, cells, width),
-                    lambda i, meta: (meta[0] * steps + i, 0, 0, 0),
+                    lambda i, meta: (lax.rem(meta[0] // slots + i, slot_total // slots), 0, 0, 0),
                 )
             ],
-            out_specs=[
-                pl.BlockSpec((slots, cells, width), lambda i, meta: (i, 0, 0)),
-                pl.BlockSpec((width, width), lambda i, meta: (0, 0)),
-            ],
+            out_specs=[out_spec(start, length) for start, length in zip(starts, steps)]
+            + [pl.BlockSpec((width, width), lambda i, meta: (0, 0))],
+            scratch_shapes=[pltpu.VMEM((slots, cells, width), jnp.bfloat16)],
         ),
-        out_shape=[
-            jax.ShapeDtypeStruct((blocks, cells, width), jnp.bfloat16),
-            jax.ShapeDtypeStruct((width, width), jnp.float32),
-        ],
+        out_shape=[jax.ShapeDtypeStruct((length, cells, width), jnp.bfloat16) for length in lens]
+        + [jax.ShapeDtypeStruct((width, width), jnp.float32)],
         compiler_params=pltpu.CompilerParams(vmem_limit_bytes=56 * 2**20),
         cost_estimate=pl.CostEstimate(
-            flops=2 * blocks * cells * width * width,
-            bytes_accessed=fine.size + fine.size // children,
+            flops=2 * total * cells * width * width,
+            bytes_accessed=4 * total * (children + 1) * cells * width,
             transcendentals=0,
         ),
     )(meta, fine)
@@ -224,9 +243,10 @@
     )(gram)
 
 
-def modes_kernel(which_ref, place_ref, split_ref, kept_ref, sent_ref, moved_ref, out_ref, rows, result, in_sem, out_sem):
+def modes_kernel(which_ref, place_ref, split_ref, *refs):
+    out_ref, rows, result, in_sem, out_sem = refs[-5:]
+    sources = refs[:-5]
     blocks, cells, width = rows.shape
-    sources = (kept_ref, sent_ref, moved_ref)
     for block in range(blocks):
         for index, source in enumerate(sources):
 
@@ -237,42 +257,46 @@
                 ).start()
 
     split = split_ref[...]
+    group = blocks // 4
     copies = []
-    for block in range(blocks):
-        pltpu.make_async_copy(kept_ref.at[0], rows.at[block], in_sem.at[block]).wait()
-        both = jnp.dot(rows[block], split, preferred_element_type=jnp.float32)
-        result[block] = (both[:, :width] + both[:, width:]).astype(jnp.bfloat16)
-        copy = pltpu.make_async_copy(
-            result.at[block], out_ref.at[pl.ds(block * cells, cells)], out_sem.at[block]
-        )
+    for first in range(0, blocks, group):
+        for block in range(first, first + group):
+            pltpu.make_async_copy(sources[0].at[0], rows.at[block], in_sem.at[block]).wait()
+        for block in range(first, first + group):
+            both = jnp.dot(rows[block], split, preferred_element_type=jnp.float32)
+            result[pl.ds(block * cells, cells), :] = (both[:, :width] + both[:, width:]).astype(
+                jnp.bfloat16
+            )
+        part = pl.ds(first * cells, group * cells)
+        copy = pltpu.make_async_copy(result.at[part], out_ref.at[part], out_sem.at[first])
         copy.start()
         copies.append(copy)
     for copy in copies:
         copy.wait()
 
 
-def make_modes(which, place, split, kept, sent, moved):
-    blocks, cells, width = kept.shape
+def make_modes(which, place, split, sources):
+    blocks, cells, width = sources[0].shape
     any_spec = pl.BlockSpec(memory_space=pl.ANY)
     smem = pl.BlockSpec(memory_space=pltpu.SMEM)
     return pl.pallas_call(
         modes_kernel,
         out_shape=jax.ShapeDtypeStruct((blocks * cells, width), jnp.bfloat16),
-        in_specs=[smem, smem, pl.BlockSpec(memory_space=pltpu.VMEM), any_spec, any_spec, any_spec],
+        in_specs=[smem, smem, pl.BlockSpec(memory_space=pltpu.VMEM)] + [any_spec] * len(sources),
         out_specs=any_spec,
         scratch_shapes=[
             pltpu.VMEM((blocks, cells, width), jnp.bfloat16),
-            pltpu.VMEM((blocks, cells, width), jnp.bfloat16),
+            pltpu.VMEM((blocks * cells, width), jnp.bfloat16),
             pltpu.SemaphoreType.DMA((blocks,)),
             pltpu.SemaphoreType.DMA((blocks,)),
         ],
-        compiler_params=pltpu.CompilerParams(vmem_limit_bytes=32 * 2**20),
+        compiler_params=pltpu.CompilerParams(vmem_limit_bytes=56 * 2**20),
         cost_estimate=pl.CostEstimate(
             flops=4 * blocks * cells * width * width,
             bytes_accessed=4 * blocks * cells * width,
             transcendentals=0,
         ),
-    )(which, place, split, kept, sent, moved)
+    )(which, place, split, *sources)
 
 
 def shards(fine, patch_count, block_place):
@@ -282,12 +306,19 @@
     parity = lax.axis_index("gy") % 2
     held_count = patch_count[0]
     send_half = 1 - parity
-    sent, sent_gram = average_half(fine, send_half, held_count)
+    early = blocks // 4
+    send_first = send_half * blocks
+    sent_a, gram_a = average_range(fine, send_first, held_count, (early,))
     pairs = [(source, source ^ 1) for source in range(lax.axis_size("gy"))]
-    moved = lax.ppermute(sent, "gy", pairs)
-    kept, kept_gram = average_half(fine, parity, held_count)
+    moved_a = lax.ppermute(sent_a, "gy", pairs)
+    sent_b, kept, gram_b = average_range(
+        fine, send_first + early, held_count, (blocks - early, blocks)
+    )
     row_total = blocks * patch_cells * lax.axis_size("gx") * lax.axis_size("gy")
-    gram = sum_everywhere(sent_gram, kept_gram, row_total)
+    moved_a, gram_b = lax.optimization_barrier((moved_a, gram_b))
+    gram = sum_everywhere(gram_a, gram_b, row_total)
+    sent_b, gram = lax.optimization_barrier((sent_b, gram))
+    moved_b = lax.ppermute(sent_b, "gy", pairs)
     factor, split = factor_and_inverse(gram)
 
     excess = jnp.where(parity == 0, held_count - blocks, blocks - held_count)
@@ -295,11 +326,12 @@
     is_moved = jnp.where(parity == 0, wanted >= blocks + excess, wanted < excess)
     own = jnp.where(parity == 0, wanted, wanted - excess)
     is_sent = own // blocks == send_half
-    which = jnp.where(is_moved, 2, jnp.where(is_sent, 1, 0)).astype(jnp.int32)
     moved_place = jnp.where(parity == 0, wanted - blocks - excess, wanted)
-    place = jnp.where(is_moved, moved_place, own % blocks)
-    place = jnp.clip(place, 0, blocks - 1).astype(jnp.int32)
-    modes = make_modes(which, place, split, kept, sent, moved)
+    place = jnp.clip(jnp.where(is_moved, moved_place, own % blocks), 0, blocks - 1)
+    late = (place >= early).astype(jnp.int32)
+    which = jnp.where(is_moved, 3 + late, jnp.where(is_sent, 1 + late, 0)).astype(jnp.int32)
+    place = jnp.where((which > 0) & (late > 0), place - early, place).astype(jnp.int32)
+    modes = make_modes(which, place, split, (kept, sent_a, sent_b, moved_a, moved_b))
     return (factor, modes)
 
 

time: 58.4 us -> 60.2 us (1.031)
  waiting for transfers between devices: 0.01 us -> 12.4 us
  Pallas kernels: 50.1 us -> 38.1 us
  starting transfers between devices: 3.02 us -> 3.74 us
    ppermute x1 -> x2, waiting for transfers between devices: 0.01 us -> 12.4 us  [the longest x1 12.4 us: shards(): moved_b = lax.ppermute(sent_b, 'gy', pairs)]
    pallas_call x1, Pallas kernels: 21.9 us -> 15.1 us  [sum_everywhere(): pl.pallas_call(functools.partial(sum_kernel, n_gx, n_gy, row_total), out_...]
    pallas_call x2, Pallas kernels: 17.1 us -> 14.4 us  [average_range(): pl.pallas_call(functools.partial(average_kernel, steps), grid_spec=pltpu....]
    pallas_call x1, Pallas kernels: 6.42 us -> 3.92 us  [make_modes(): pl.pallas_call(modes_kernel, out_shape=jax.ShapeDtypeStruct((blocks * cel...]
    ppermute x1 -> x2, starting transfers between devices: 3.02 us -> 3.74 us  [the longest x1 3.02 us: shards(): moved_a = lax.ppermute(sent_a, 'gy', pairs)]
    unnamed x8 -> x10, local copies, waits for them, and re-layouts: 2.06 us -> 2.34 us
  transfers between devices with their start and end apart: 1 -> 2, of which waited for: 0 -> 1; matrix products, arithmetic and copies ran while one was open for 1% -> 2% of each run, Pallas kernels for 61% -> 26%
where the time goes in v2:
time: 60.2 us; the launch traced here: 59.7 us
  Pallas kernels  38.1 us (63%)
  waiting for transfers between devices  12.4 us (21%)
  starting transfers between devices  3.74 us (6%)
  local copies, waits for them, and re-layouts  2.34 us (4%)
  other arithmetic  1.85 us (3%)
  between operations  1.32 us (2%)
    pallas_call x1, Pallas kernels, sum_everywhere(): pl.pallas_call(functools.partial(sum_kernel, n_gx, n_gy, row_total), out_...  15.1 us
    pallas_call x2, Pallas kernels, average_range(): pl.pallas_call(functools.partial(average_kernel, steps), grid_spec=pltpu....  14.4 us
    ppermute x1, waiting for transfers between devices, shards(): moved_b = lax.ppermute(sent_b, 'gy', pairs)  12.4 us
    pallas_call x1, Pallas kernels, factor_and_inverse(): pl.pallas_call(factor_kernel, out_shape=[jax.ShapeDtypeStruct((width, wid...  4.63 us
    pallas_call x1, Pallas kernels, make_modes(): pl.pallas_call(modes_kernel, out_shape=jax.ShapeDtypeStruct((blocks * cel...  3.92 us
    ppermute x1, starting transfers between devices, shards(): moved_a = lax.ppermute(sent_a, 'gy', pairs)  3.02 us
    unnamed x10, local copies, waits for them, and re-layouts  2.34 us
    another operation x2, other arithmetic, average_range(): meta = jnp.stack([first, count, jnp.int32(slot_total)])  1.27 us
  transfers between devices with their start and end apart: 2, of which 1 were waited for; matrix products, arithmetic and copies ran while one was open for 2% of the time, Pallas kernels for 26%

profile of v2, /device:TPU:0, one launch (start us, length us, event | category | flops | bytes accessed | tf_op | source)
XLA Modules:
  0.0 59.7 jit_solution(15947892557728725751)
XLA Ops:
  1.3 0.6 %pad_add_fusion.meta_ref = s32[3]{0:T(128)} fusion(s32[1]{0:T(128)} %constant.56.clone.1, s32[1]{0:T(128)} %bitcast.1, s32[1]{0:T(128)S(6)} %copy.5), kind=kLoop, calls=%fused_computation.11 | loop fusion | flops 6 | bytes 24 | tf_op jit(solution)/shard_map/stack | solution.py:58
  1.9 0.0 copy-start.4
  1.9 3.6 %shard_map.51 = (bf16[4,256,128]{2,1,0:T(8,128)(2,1)}, f32[128,128]{1,0:T(8,128)}) custom-call(s32[3]{0:T(128)} %pad_add_fusion.meta_ref, bf16[32,8,256,128]{3,2,1,0:T(8,128)(2,1)} %fine_ref.3), custom_call_target="tpu_custom_call" | custom-call | flops 33554432 | bytes 4718592 | tf_op jit(solution)/shard_map/pallas_call | solution.py:65
  5.5 3.0 %collective-permute-start = (bf16[4,256,128]{2,1,0:T(8,128)(2,1)}, bf16[4,256,128]{2,1,0:T(8,128)(2,1)S(1)}, u32[]{:S(2)}, u32[]{:S(2)}) collective-permute-start(bf16[4,256,128]{2,1,0:T(8,128)(2,1)} %get-tuple-element.15.refs_1_), channel_id=1, source_target_pairs={{0,1},{1,0},{2,3},{3,2},{4,5},{5,4},{6,7},{7,6},{8,9},{9,8},{10,11... | collective-permute-start | bytes 786440 | tf_op jit(solution)/shard_map/ppermute | solution.py:313
  8.6 0.7 %pad_add_fusion.1.meta_ref = s32[3]{0:T(128)} fusion(s32[1]{0:T(128)} %constant.56.clone.1, s32[1]{0:T(128)} %bitcast, s32[1]{0:T(128)S(6)} %copy.5), kind=kLoop, calls=%fused_computation.12 | loop fusion | flops 6 | bytes 24 | tf_op jit(solution)/shard_map/stack | solution.py:58
  9.2 10.7 %shard_map.50 = (bf16[12,256,128]{2,1,0:T(8,128)(2,1)}, bf16[16,256,128]{2,1,0:T(8,128)(2,1)}, f32[128,128]{1,0:T(8,128)}) custom-call(s32[3]{0:T(128)} %pad_add_fusion.1.meta_ref, bf16[32,8,256,128]{3,2,1,0:T(8,128)(2,1)} %fine_ref.3), custom_call_target="tpu_custom_call" | custom-call | flops 234881024 | bytes 33030144 | tf_op jit(solution)/shard_map/pallas_call | solution.py:65
  20.0 0.0 collective-permute-done.refs_3_
  20.0 0.0 copy-start.3
  20.0 15.1 %shard_map.52.gram_ref = f32[128,128]{1,0:T(8,128)} custom-call(f32[128,128]{1,0:T(8,128)} %get-tuple-element.14.first_ref, f32[128,128]{1,0:T(8,128)} %get-tuple-element.17.second_ref), custom_call_target="tpu_custom_call" | custom-call | bytes 33554432 | tf_op jit(solution)/shard_map/pallas_call | solution.py:168
  35.1 0.7 %collective-permute-start.1 = (bf16[12,256,128]{2,1,0:T(8,128)(2,1)}, bf16[12,256,128]{2,1,0:T(8,128)(2,1)S(1)}, u32[]{:S(2)}, u32[]{:S(2)}) collective-permute-start(bf16[12,256,128]{2,1,0:T(8,128)(2,1)} %get-tuple-element.22.refs_2_), channel_id=1, source_target_pairs={{0,1},{1,0},{2,3},{3,2},{4,5},{5,4},{6,7},{7,6},{8,9},{9,8},{10,11... | collective-permute-start | bytes 2359304 | tf_op jit(solution)/shard_map/ppermute | solution.py:321
  35.8 0.0 copy-done.4
  35.8 0.6 and_select_fusion
  36.4 0.0 copy-start
  36.4 0.8 %copy-done = f32[128,128]{1,0:T(8,128)S(1)} copy-done((f32[128,128]{1,0:T(8,128)S(1)}, f32[128,128]{1,0:T(8,128)}, u32[]{:S(2)}) %copy-start) | copy-done | bytes 65560
  37.3 4.6 %shard_map.53 = (f32[128,128]{1,0:T(8,128)}, bf16[128,256]{1,0:T(8,128)(2,1)S(1)}) custom-call(f32[128,128]{1,0:T(8,128)S(1)} %copy-done), custom_call_target="tpu_custom_call" | custom-call | bytes 33554432 | tf_op jit(solution)/shard_map/pallas_call | solution.py:233
  41.9 0.0 copy-start.1
  41.9 0.6 %copy-done.1 = bf16[128,256]{1,0:T(8,128)(2,1)} copy-done((bf16[128,256]{1,0:T(8,128)(2,1)}, bf16[128,256]{1,0:T(8,128)(2,1)S(1)}, u32[]{:S(2)}) %copy-start.1) | copy-done | bytes 65560
  42.5 12.4 %collective-permute-done.1.refs_4_ = bf16[12,256,128]{2,1,0:T(8,128)(2,1)S(1)} collective-permute-done((bf16[12,256,128]{2,1,0:T(8,128)(2,1)}, bf16[12,256,128]{2,1,0:T(8,128)(2,1)S(1)}, u32[]{:S(2)}, u32[]{:S(2)}) %collective-permute-start.1) | collective-permute-done | bytes 786464 | tf_op jit(solution)/shard_map/ppermute | solution.py:321
  54.9 0.0 copy-start.2
  54.9 0.0 copy-done.3
  55.0 0.9 %copy-done.2 = bf16[12,256,128]{2,1,0:T(8,128)(2,1)} copy-done((bf16[12,256,128]{2,1,0:T(8,128)(2,1)}, bf16[12,256,128]{2,1,0:T(8,128)(2,1)S(1)}, u32[]{:S(2)}) %copy-start.2) | copy-done | bytes 786456
  55.8 3.9 %shard_map.54 = bf16[4096,128]{1,0:T(8,128)(2,1)} custom-call(s32[16]{0:T(128)} %get-tuple-element.25.which_ref, s32[16]{0:T(128)} %get-tuple-element.24.place_ref, bf16[128,256]{1,0:T(8,128)(2,1)} %copy-done.1, bf16[16,256,128]{2,1,0:T(8,128)(2,1)} %get-tuple-element.21.refs_0_, bf16[4,256,128]{2,1,0:T(8,128)(2,1)} %get-tuple-element.15.refs_1_, ...), custom_call_target="tpu_custom_call" | custom-call | flops 268435456 | bytes 2097152 | tf_op jit(solution)/shard_map/pallas_call | solution.py:282
Async XLA Ops:
  1.9 33.9 %copy-start.4 = (s32[1,16]{1,0:T(1,128)S(1)}, s32[1,16]{1,0:T(1,128)}, u32[]{:S(2)}) copy-start(s32[1,16]{1,0:T(1,128)} %param.5) | copy-start | bytes 196
  5.5 14.4 %collective-permute-start = (bf16[4,256,128]{2,1,0:T(8,128)(2,1)}, bf16[4,256,128]{2,1,0:T(8,128)(2,1)S(1)}, u32[]{:S(2)}, u32[]{:S(2)}) collective-permute-start(bf16[4,256,128]{2,1,0:T(8,128)(2,1)} %get-tuple-element.15.refs_1_), channel_id=1, source_target_pairs={{0,1},{1,0},{2,3},{3,2},{4,5},{5,4},{6,7},{7,6},{8,9},{9,8},{10,11... | collective-permute-start | bytes 786440 | tf_op jit(solution)/shard_map/ppermute | solution.py:313
  20.0 35.0 %copy-start.3 = (bf16[4,256,128]{2,1,0:T(8,128)(2,1)}, bf16[4,256,128]{2,1,0:T(8,128)(2,1)S(1)}, u32[]{:S(2)}) copy-start(bf16[4,256,128]{2,1,0:T(8,128)(2,1)S(1)} %collective-permute-done.refs_3_) | copy-start | bytes 786436
  35.1 19.8 %collective-permute-start.1 = (bf16[12,256,128]{2,1,0:T(8,128)(2,1)}, bf16[12,256,128]{2,1,0:T(8,128)(2,1)S(1)}, u32[]{:S(2)}, u32[]{:S(2)}) collective-permute-start(bf16[12,256,128]{2,1,0:T(8,128)(2,1)} %get-tuple-element.22.refs_2_), channel_id=1, source_target_pairs={{0,1},{1,0},{2,3},{3,2},{4,5},{5,4},{6,7},{7,6},{8,9},{9,8},{10,11... | collective-permute-start | bytes 2359304 | tf_op jit(solution)/shard_map/ppermute | solution.py:321
  36.4 0.8 %copy-start = (f32[128,128]{1,0:T(8,128)S(1)}, f32[128,128]{1,0:T(8,128)}, u32[]{:S(2)}) copy-start(f32[128,128]{1,0:T(8,128)} %shard_map.52.gram_ref) | copy-start | bytes 196612
  41.9 0.6 %copy-start.1 = (bf16[128,256]{1,0:T(8,128)(2,1)}, bf16[128,256]{1,0:T(8,128)(2,1)S(1)}, u32[]{:S(2)}) copy-start(bf16[128,256]{1,0:T(8,128)(2,1)S(1)} %get-tuple-element.20.split_ref) | copy-start | bytes 196612
  54.9 0.9 %copy-start.2 = (bf16[12,256,128]{2,1,0:T(8,128)(2,1)}, bf16[12,256,128]{2,1,0:T(8,128)(2,1)S(1)}, u32[]{:S(2)}) copy-start(bf16[12,256,128]{2,1,0:T(8,128)(2,1)S(1)} %collective-permute-done.1.refs_4_) | copy-start | bytes 2359300

commit v3 on v2

--- a/solution.py
+++ b/solution.py
@@ -10,7 +10,7 @@
 MESH = pl.DeviceIdType.MESH
 
 
-def average_kernel(lens, meta_ref, fine_ref, *refs):
+def average_kernel(lens, offset, meta_ref, fine_ref, *refs):
     step = pl.program_id(0)
     slots, children, cells, width = fine_ref.shape
     outs, gram_ref, masked = refs[: len(lens)], refs[-2], refs[-1]
@@ -23,7 +23,7 @@
         piece = 32
         acc = None
         for slot in range(slots):
-            number = lax.rem(meta_ref[0] + step * slots + slot, meta_ref[2])
+            number = lax.rem(meta_ref[0] + offset + step * slots + slot, meta_ref[2])
             weight = jnp.where(number < meta_ref[1], 1.0, 0.0).astype(jnp.float32)
             for row in range(0, cells, piece):
                 rows = pl.ds(row, piece)
@@ -49,13 +49,12 @@
         start += length
 
 
-def average_range(fine, first, count, lens):
+def average_range(fine, meta, offset, lens):
     slot_total, children, cells, width = fine.shape
     slots = slot_total // 8
     total = sum(lens)
     steps = [length // slots for length in lens]
     starts = [sum(steps[:k]) for k in range(len(steps))]
-    meta = jnp.stack([first, count, jnp.int32(slot_total)])
 
     def out_spec(start, length):
         return pl.BlockSpec(
@@ -63,14 +62,14 @@
         )
 
     return pl.pallas_call(
-        functools.partial(average_kernel, steps),
+        functools.partial(average_kernel, steps, offset),
         grid_spec=pltpu.PrefetchScalarGridSpec(
             num_scalar_prefetch=1,
             grid=(sum(steps),),
             in_specs=[
                 pl.BlockSpec(
                     (slots, children, cells, width),
-                    lambda i, meta: (lax.rem(meta[0] // slots + i, slot_total // slots), 0, 0, 0),
+                    lambda i, meta: (lax.rem(meta[0] // slots + offset // slots + i, slot_total // slots), 0, 0, 0),
                 )
             ],
             out_specs=[out_spec(start, length) for start, length in zip(starts, steps)]
@@ -178,7 +177,7 @@
             pltpu.SemaphoreType.DMA((3, most)),
         ],
         compiler_params=pltpu.CompilerParams(collective_id=0, has_side_effects=True),
-        cost_estimate=pl.CostEstimate(flops=0, bytes_accessed=32 * 2**20, transcendentals=0),
+        cost_estimate=pl.CostEstimate(flops=0, bytes_accessed=2**18, transcendentals=0),
     )(first, second)
 
 
@@ -306,18 +305,16 @@
     parity = lax.axis_index("gy") % 2
     held_count = patch_count[0]
     send_half = 1 - parity
-    early = blocks // 4
+    early = 3 * blocks // 4
     send_first = send_half * blocks
-    sent_a, gram_a = average_range(fine, send_first, held_count, (early,))
+    meta = jnp.stack([send_first, held_count, jnp.int32(slot_total)])
+    sent_a, gram_a = average_range(fine, meta, 0, (early,))
     pairs = [(source, source ^ 1) for source in range(lax.axis_size("gy"))]
     moved_a = lax.ppermute(sent_a, "gy", pairs)
-    sent_b, kept, gram_b = average_range(
-        fine, send_first + early, held_count, (blocks - early, blocks)
-    )
+    sent_b, kept, gram_b = average_range(fine, meta, early, (blocks - early, blocks))
     row_total = blocks * patch_cells * lax.axis_size("gx") * lax.axis_size("gy")
-    moved_a, gram_b = lax.optimization_barrier((moved_a, gram_b))
     gram = sum_everywhere(gram_a, gram_b, row_total)
-    sent_b, gram = lax.optimization_barrier((sent_b, gram))
+    sent_b, gram, moved_a = lax.optimization_barrier((sent_b, gram, moved_a))
     moved_b = lax.ppermute(sent_b, "gy", pairs)
     factor, split = factor_and_inverse(gram)
 

time: 60.2 us -> 50.1 us (0.83)
  waiting for transfers between devices: 12.4 us -> 1.21 us
  Pallas kernels: 38.1 us -> 39.9 us
  other arithmetic: 1.85 us -> 1.24 us
    ppermute x1, waiting for transfers between devices: 12.4 us -> 1.21 us  [shards(): moved_b = lax.ppermute(sent_b, 'gy', pairs)]
    pallas_call x1, Pallas kernels: 15.1 us -> 17.1 us  [sum_everywhere(): pl.pallas_call(functools.partial(sum_kernel, n_gx, n_gy, row_total), out_...]
    another operation x2 -> x1, other arithmetic: 1.27 us -> 0.65 us  [shards(): meta = jnp.stack([send_first, held_count, jnp.int32(slot_total)])]
  transfers between devices with their start and end apart: 2 -> 2, of which waited for: 1 -> 1; matrix products, arithmetic and copies ran while one was open for 2% -> 1% of each run, Pallas kernels for 26% -> 61%
where the time goes in v3:
time: 50.1 us; the launch traced here: 49.6 us
  Pallas kernels  39.9 us (80%)
  starting transfers between devices  3.74 us (7%)
  local copies, waits for them, and re-layouts  2.16 us (4%)
  between operations  1.32 us (3%)
  other arithmetic  1.24 us (2%)
  waiting for transfers between devices  1.21 us (2%)
    pallas_call x1, Pallas kernels, sum_everywhere(): pl.pallas_call(functools.partial(sum_kernel, n_gx, n_gy, row_total), out_...  17.1 us
    pallas_call x2, Pallas kernels, average_range(): pl.pallas_call(functools.partial(average_kernel, steps, offset), grid_spe...  14.2 us
    pallas_call x1, Pallas kernels, factor_and_inverse(): pl.pallas_call(factor_kernel, out_shape=[jax.ShapeDtypeStruct((width, wid...  4.63 us
    pallas_call x1, Pallas kernels, make_modes(): pl.pallas_call(modes_kernel, out_shape=jax.ShapeDtypeStruct((blocks * cel...  3.92 us
    ppermute x1, starting transfers between devices, shards(): moved_a = lax.ppermute(sent_a, 'gy', pairs)  3.02 us
    unnamed x10, local copies, waits for them, and re-layouts  2.16 us
    ppermute x1, waiting for transfers between devices, shards(): moved_b = lax.ppermute(sent_b, 'gy', pairs)  1.21 us
  transfers between devices with their start and end apart: 2, of which 1 were waited for; matrix products, arithmetic and copies ran while one was open for 1% of the time, Pallas kernels for 61%

profile of v3, /device:TPU:0, one launch (start us, length us, event | category | flops | bytes accessed | tf_op | source)
XLA Modules:
  0.0 49.6 jit_solution(17894317047275815888)
XLA Ops:
  1.3 0.7 %pad_add_fusion.meta_ref = s32[3]{0:T(128)} fusion(s32[1]{0:T(128)} %constant.54.clone.1, s32[1]{0:T(128)S(6)} %copy.5, s32[1]{0:T(128)} %bitcast), kind=kLoop, calls=%fused_computation.13 | loop fusion | flops 6 | bytes 24 | tf_op jit(solution)/shard_map/stack | solution.py:310
  1.9 0.0 copy-start.4
  1.9 6.0 %shard_map.51 = (bf16[12,256,128]{2,1,0:T(8,128)(2,1)}, f32[128,128]{1,0:T(8,128)}) custom-call(s32[3]{0:T(128)} %pad_add_fusion.meta_ref, bf16[32,8,256,128]{3,2,1,0:T(8,128)(2,1)} %fine_ref.3), custom_call_target="tpu_custom_call" | custom-call | flops 100663296 | bytes 14155776 | tf_op jit(solution)/shard_map/pallas_call | solution.py:64
  7.9 3.0 %collective-permute-start = (bf16[12,256,128]{2,1,0:T(8,128)(2,1)}, bf16[12,256,128]{2,1,0:T(8,128)(2,1)S(1)}, u32[]{:S(2)}, u32[]{:S(2)}) collective-permute-start(bf16[12,256,128]{2,1,0:T(8,128)(2,1)} %get-tuple-element.15.refs_1_), channel_id=1, source_target_pairs={{0,1},{1,0},{2,3},{3,2},{4,5},{5,4},{6,7},{7,6},{8,9},{9,8},{10,11... | collective-permute-start | bytes 2359304 | tf_op jit(solution)/shard_map/ppermute | solution.py:313
  10.9 8.3 %shard_map.50 = (bf16[4,256,128]{2,1,0:T(8,128)(2,1)}, bf16[16,256,128]{2,1,0:T(8,128)(2,1)}, f32[128,128]{1,0:T(8,128)}) custom-call(s32[3]{0:T(128)} %pad_add_fusion.meta_ref, bf16[32,8,256,128]{3,2,1,0:T(8,128)(2,1)} %fine_ref.3), custom_call_target="tpu_custom_call" | custom-call | flops 167772160 | bytes 23592960 | tf_op jit(solution)/shard_map/pallas_call | solution.py:64
  19.2 17.1 %shard_map.52.gram_ref = f32[128,128]{1,0:T(8,128)} custom-call(f32[128,128]{1,0:T(8,128)} %get-tuple-element.13.first_ref, f32[128,128]{1,0:T(8,128)} %get-tuple-element.14.second_ref), custom_call_target="tpu_custom_call" | custom-call | bytes 262144 | tf_op jit(solution)/shard_map/pallas_call | solution.py:167
  36.4 0.0 collective-permute-done.refs_3_
  36.4 0.0 copy-start.2
  36.4 0.7 %collective-permute-start.1 = (bf16[4,256,128]{2,1,0:T(8,128)(2,1)}, bf16[4,256,128]{2,1,0:T(8,128)(2,1)S(1)}, u32[]{:S(2)}, u32[]{:S(2)}) collective-permute-start(bf16[4,256,128]{2,1,0:T(8,128)(2,1)} %get-tuple-element.20.refs_2_), channel_id=1, source_target_pairs={{0,1},{1,0},{2,3},{3,2},{4,5},{5,4},{6,7},{7,6},{8,9},{9,8},{10,11... | collective-permute-start | bytes 786440 | tf_op jit(solution)/shard_map/ppermute | solution.py:318
  37.1 0.0 copy-done.4
  37.1 0.6 %and_select_fusion = (s32[16]{0:T(128)}, s32[16]{0:T(128)}) fusion(s32[]{:T(128)S(6)} %sub.32, s32[]{:T(128)S(6)} %select_n.54, s32[]{:T(128)S(6)} %add.25, s32[1,16]{1,0:T(1,128)S(1)} %copy-done.4, pred[]{:T(512)S(6)} %eq.16), kind=kLoop, calls=%fused_computation | loop fusion | flops 656 | bytes 205 | tf_op jit(solution)/shard_map/jit(_where)/select_n | solution.py:330
  37.7 0.0 copy-start
  37.7 0.8 %copy-done = f32[128,128]{1,0:T(8,128)S(1)} copy-done((f32[128,128]{1,0:T(8,128)S(1)}, f32[128,128]{1,0:T(8,128)}, u32[]{:S(2)}) %copy-start) | copy-done | bytes 65560
  38.5 4.6 %shard_map.53 = (f32[128,128]{1,0:T(8,128)}, bf16[128,256]{1,0:T(8,128)(2,1)S(1)}) custom-call(f32[128,128]{1,0:T(8,128)S(1)} %copy-done), custom_call_target="tpu_custom_call" | custom-call | bytes 33554432 | tf_op jit(solution)/shard_map/pallas_call | solution.py:232
  43.2 0.0 copy-start.1
  43.2 0.6 %copy-done.1 = bf16[128,256]{1,0:T(8,128)(2,1)} copy-done((bf16[128,256]{1,0:T(8,128)(2,1)}, bf16[128,256]{1,0:T(8,128)(2,1)S(1)}, u32[]{:S(2)}) %copy-start.1) | copy-done | bytes 65560
  43.8 1.2 %collective-permute-done.1.refs_4_ = bf16[4,256,128]{2,1,0:T(8,128)(2,1)S(1)} collective-permute-done((bf16[4,256,128]{2,1,0:T(8,128)(2,1)}, bf16[4,256,128]{2,1,0:T(8,128)(2,1)S(1)}, u32[]{:S(2)}, u32[]{:S(2)}) %collective-permute-start.1) | collective-permute-done | bytes 262176 | tf_op jit(solution)/shard_map/ppermute | solution.py:318
  45.0 0.0 copy-start.3
  45.0 0.0 copy-done.2
  45.0 0.7 %copy-done.3 = bf16[4,256,128]{2,1,0:T(8,128)(2,1)} copy-done((bf16[4,256,128]{2,1,0:T(8,128)(2,1)}, bf16[4,256,128]{2,1,0:T(8,128)(2,1)S(1)}, u32[]{:S(2)}) %copy-start.3) | copy-done | bytes 262168
  45.7 3.9 %shard_map.54 = bf16[4096,128]{1,0:T(8,128)(2,1)} custom-call(s32[16]{0:T(128)} %get-tuple-element.23.which_ref, s32[16]{0:T(128)} %get-tuple-element.22.place_ref, bf16[128,256]{1,0:T(8,128)(2,1)} %copy-done.1, bf16[16,256,128]{2,1,0:T(8,128)(2,1)} %get-tuple-element.19.refs_0_, bf16[12,256,128]{2,1,0:T(8,128)(2,1)} %get-tuple-element.15.refs_1_, ...), custom_call_target="tpu_custom_call" | custom-call | flops 268435456 | bytes 2097152 | tf_op jit(solution)/shard_map/pallas_call | solution.py:281
Async XLA Ops:
  1.9 35.2 %copy-start.4 = (s32[1,16]{1,0:T(1,128)S(1)}, s32[1,16]{1,0:T(1,128)}, u32[]{:S(2)}) copy-start(s32[1,16]{1,0:T(1,128)} %param.5) | copy-start | bytes 196
  7.9 28.5 %collective-permute-start = (bf16[12,256,128]{2,1,0:T(8,128)(2,1)}, bf16[12,256,128]{2,1,0:T(8,128)(2,1)S(1)}, u32[]{:S(2)}, u32[]{:S(2)}) collective-permute-start(bf16[12,256,128]{2,1,0:T(8,128)(2,1)} %get-tuple-element.15.refs_1_), channel_id=1, source_target_pairs={{0,1},{1,0},{2,3},{3,2},{4,5},{5,4},{6,7},{7,6},{8,9},{9,8},{10,11... | collective-permute-start | bytes 2359304 | tf_op jit(solution)/shard_map/ppermute | solution.py:313
  36.4 8.6 %copy-start.2 = (bf16[12,256,128]{2,1,0:T(8,128)(2,1)}, bf16[12,256,128]{2,1,0:T(8,128)(2,1)S(1)}, u32[]{:S(2)}) copy-start(bf16[12,256,128]{2,1,0:T(8,128)(2,1)S(1)} %collective-permute-done.refs_3_) | copy-start | bytes 2359300
  36.4 8.6 %collective-permute-start.1 = (bf16[4,256,128]{2,1,0:T(8,128)(2,1)}, bf16[4,256,128]{2,1,0:T(8,128)(2,1)S(1)}, u32[]{:S(2)}, u32[]{:S(2)}) collective-permute-start(bf16[4,256,128]{2,1,0:T(8,128)(2,1)} %get-tuple-element.20.refs_2_), channel_id=1, source_target_pairs={{0,1},{1,0},{2,3},{3,2},{4,5},{5,4},{6,7},{7,6},{8,9},{9,8},{10,11... | collective-permute-start | bytes 786440 | tf_op jit(solution)/shard_map/ppermute | solution.py:318
  37.7 0.8 %copy-start = (f32[128,128]{1,0:T(8,128)S(1)}, f32[128,128]{1,0:T(8,128)}, u32[]{:S(2)}) copy-start(f32[128,128]{1,0:T(8,128)} %shard_map.52.gram_ref) | copy-start | bytes 196612
  43.2 0.6 %copy-start.1 = (bf16[128,256]{1,0:T(8,128)(2,1)}, bf16[128,256]{1,0:T(8,128)(2,1)S(1)}, u32[]{:S(2)}) copy-start(bf16[128,256]{1,0:T(8,128)(2,1)S(1)} %get-tuple-element.18.split_ref) | copy-start | bytes 196612
  45.0 0.7 %copy-start.3 = (bf16[4,256,128]{2,1,0:T(8,128)(2,1)}, bf16[4,256,128]{2,1,0:T(8,128)(2,1)S(1)}, u32[]{:S(2)}) copy-start(bf16[4,256,128]{2,1,0:T(8,128)(2,1)S(1)} %collective-permute-done.1.refs_4_) | copy-start | bytes 786436
